TPU v7x, 32 devices: a whole 2x2x4 slice. The times are simulated.
32 devices in a mesh: dp: 32 (over z, y, x, core).
Axes of the slice: x: 2, y: 2, z: 4, core: 2. Of those that a mesh axis runs over, the one named last changes fastest.
Arguments:
- tokens: bfloat16 [16384, 768], P('dp'), may hold values from -6 to 6
- cotangent: bfloat16 [16384, 768], P('dp'), may hold values from -6 to 6
- seq_len: int32 [32], P('dp'), may hold values from 64 to 512, as said below
- ln1_gain: bfloat16 [2, 768], P(None, 'dp'), may hold values from 0.5 to 1.5
- ln1_bias: bfloat16 [2, 768], P(None, 'dp'), may hold values from -3 to 3
- qkv_weight: bfloat16 [2, 768, 2304], P(None, 'dp'), may hold values from -0.21875 to 0.21875
- qv_bias: bfloat16 [2, 1536], P(None, 'dp'), may hold values from -3 to 3
- out_weight: bfloat16 [2, 768, 768], P(None, 'dp'), may hold values from -1.75 to 1.75
- out_bias: bfloat16 [2, 768], P(None, 'dp'), may hold values from -3 to 3
- ln2_gain: bfloat16 [2, 768], P(None, 'dp'), may hold values from 0.5 to 1.5
- ln2_bias: bfloat16 [2, 768], P(None, 'dp'), may hold values from -3 to 3
- fc_weight: bfloat16 [2, 768, 3072], P(None, 'dp'), may hold values from -0.21875 to 0.21875
- fc_bias: bfloat16 [2, 3072], P(None, 'dp'), may hold values from -3 to 3
- proj_weight: bfloat16 [2, 3072, 768], P(None, 'dp'), may hold values from -0.109375 to 0.109375
- proj_bias: bfloat16 [2, 768], P(None, 'dp'), may hold values from -3 to 3
Outputs:
- output: bfloat16 [16384, 768], P('dp')
- tokens_grad: bfloat16 [16384, 768], P('dp')
- ln1_gain_grad: float32 [2, 768], P(None, 'dp')
- ln1_bias_grad: float32 [2, 768], P(None, 'dp')
- qkv_weight_grad: float32 [2, 768, 2304], P(None, 'dp')
- qv_bias_grad: float32 [2, 1536], P(None, 'dp')
- out_weight_grad: float32 [2, 768, 768], P(None, 'dp')
- out_bias_grad: float32 [2, 768], P(None, 'dp')
- ln2_gain_grad: float32 [2, 768], P(None, 'dp')
- ln2_bias_grad: float32 [2, 768], P(None, 'dp')
- fc_weight_grad: float32 [2, 768, 3072], P(None, 'dp')
- fc_bias_grad: float32 [2, 3072], P(None, 'dp')
- proj_weight_grad: float32 [2, 3072, 768], P(None, 'dp')
- proj_bias_grad: float32 [2, 768], P(None, 'dp')
Inputs may be any that keep to these rules, and one draw needn't show every extreme that they name: `seq_len`: each sequence has 64 to 512 live tokens; some sequence has exactly 512.
All inputs are finite; a program needn't handle non-finite values.
Results may differ from a plain program's by a relative error of at most 0.015.
Values may be sent and summed in bfloat16 or wider, within the bound.
A program may use at most 320 MiB of HBM per device.

v0:
```python
import math

import jax
import jax.numpy as jnp
from jax import lax
from jax.sharding import PartitionSpec as P

D = 768
HD = 64
SEQ = 512
LAYERS = 2


eps = 1e-05


def norm_stats(rows):
    mean = jnp.mean(rows, axis=-1, keepdims=True)
    centred = rows - mean
    var = jnp.mean(centred * centred, axis=-1, keepdims=True)
    inverse = lax.rsqrt(var + eps)
    return (centred * inverse, inverse)


def norm_back(grad_hat, hat, inverse):
    first = jnp.mean(grad_hat, axis=-1, keepdims=True)
    second = jnp.mean(grad_hat * hat, axis=-1, keepdims=True)
    return inverse * (grad_hat - first - hat * second)


def allowed_pairs(length):
    place = jnp.arange(SEQ, dtype=jnp.int32)
    return (place[None, :] <= place[:, None]) & (place[None, :] < length)


def to_blocks(matrix, slots):
    half = matrix.shape[1] // 2
    return matrix.reshape(slots, SEQ, 2, half).transpose(0, 2, 1, 3).reshape(slots * 2, SEQ, half)


def from_blocks(blocks, slots):
    half = blocks.shape[2]
    return blocks.reshape(slots, 2, SEQ, half).transpose(0, 2, 1, 3).reshape(slots * SEQ, 2 * half)


def attend_block(item):
    query, keys, values, length = item
    heads = query.shape[1] // HD
    q_heads = query.reshape(SEQ, heads, HD)
    k_heads = keys.reshape(SEQ, heads, HD)
    v_heads = values.reshape(SEQ, heads, HD)
    scores = jnp.einsum("qhd,khd->hqk", q_heads, k_heads, preferred_element_type=jnp.float32) * (
        1.0 / math.sqrt(HD)
    )
    scores = jnp.where(allowed_pairs(length)[None], scores, -1e30)
    top = jnp.max(scores, axis=-1, keepdims=True)
    expo = jnp.exp(scores - top)
    total = jnp.sum(expo, axis=-1, keepdims=True)
    probs = (expo / total).astype(jnp.bfloat16)
    attended = jnp.einsum("hqk,khd->qhd", probs, v_heads, preferred_element_type=jnp.float32)
    return (attended.reshape(SEQ, heads * HD).astype(jnp.bfloat16), top + jnp.log(total))


def attend_back(item):
    query, keys, values, length, lse, grad_out = item
    heads = query.shape[1] // HD
    q_heads = query.reshape(SEQ, heads, HD)
    k_heads = keys.reshape(SEQ, heads, HD)
    v_heads = values.reshape(SEQ, heads, HD)
    g_heads = grad_out.reshape(SEQ, heads, HD)
    scale = 1.0 / math.sqrt(HD)
    scores = (
        jnp.einsum("qhd,khd->hqk", q_heads, k_heads, preferred_element_type=jnp.float32) * scale
    )
    allowed = allowed_pairs(length)[None]
    scores = jnp.where(allowed, scores, -1e30)
    probs = jnp.exp(scores - lse)
    grad_probs = jnp.einsum("qhd,khd->hqk", g_heads, v_heads, preferred_element_type=jnp.float32)
    delta = jnp.sum(probs * grad_probs, axis=-1, keepdims=True)
    grad_scores = jnp.where(allowed, probs * (grad_probs - delta), 0.0).astype(jnp.bfloat16)
    grad_query = (
        jnp.einsum("hqk,khd->qhd", grad_scores, k_heads, preferred_element_type=jnp.float32) * scale
    )
    grad_keys = (
        jnp.einsum("hqk,qhd->khd", grad_scores, q_heads, preferred_element_type=jnp.float32) * scale
    )
    grad_values = jnp.einsum(
        "hqk,qhd->khd", probs.astype(jnp.bfloat16), g_heads, preferred_element_type=jnp.float32
    )
    width = heads * HD
    return (
        grad_query.reshape(SEQ, width).astype(jnp.bfloat16),
        grad_keys.reshape(SEQ, width).astype(jnp.bfloat16),
        grad_values.reshape(SEQ, width).astype(jnp.bfloat16),
    )


def forward_layer(state, weights, lengths):
    ln1_g, ln1_b, w_qkv, b_qv, w_out, b_out, ln2_g, ln2_b, w_fc, b_fc, w_proj, b_proj = weights
    slots = lengths.shape[0]
    hat1, inverse1 = norm_stats(state)
    normed = (hat1 * ln1_g + ln1_b).astype(jnp.bfloat16)
    qkv = jnp.dot(normed, w_qkv, preferred_element_type=jnp.float32)
    query = (qkv[:, :D] + b_qv[:D]).astype(jnp.bfloat16)
    keys = qkv[:, D : 2 * D].astype(jnp.bfloat16)
    values = (qkv[:, 2 * D :] + b_qv[D:]).astype(jnp.bfloat16)
    block_lengths = jnp.repeat(lengths, 2)
    att_blocks, lse = lax.map(
        attend_block,
        (to_blocks(query, slots), to_blocks(keys, slots), to_blocks(values, slots), block_lengths),
    )
    attended = from_blocks(att_blocks, slots)
    middle = state + jnp.dot(attended, w_out, preferred_element_type=jnp.float32) + b_out
    hat2, inverse2 = norm_stats(middle)
    normed2 = (hat2 * ln2_g + ln2_b).astype(jnp.bfloat16)
    pre = jnp.dot(normed2, w_fc, preferred_element_type=jnp.float32) + b_fc
    act = jax.nn.gelu(pre, approximate=True).astype(jnp.bfloat16)
    result = middle + jnp.dot(act, w_proj, preferred_element_type=jnp.float32) + b_proj
    kept = (
        hat1,
        inverse1,
        normed,
        query,
        keys,
        values,
        attended,
        lse,
        hat2,
        inverse2,
        normed2,
        pre,
        act,
    )
    return (result, kept)


def column_sums(matrix):
    return jnp.sum(matrix.astype(jnp.float32), axis=0)


def backward_layer(grad, weights, kept, lengths):
    ln1_g, ln1_b, w_qkv, b_qv, w_out, b_out, ln2_g, ln2_b, w_fc, b_fc, w_proj, b_proj = weights
    (
        hat1,
        inverse1,
        normed,
        query,
        keys,
        values,
        attended,
        lse,
        hat2,
        inverse2,
        normed2,
        pre,
        act,
    ) = kept
    slots = lengths.shape[0]
    grad_mlp = grad.astype(jnp.bfloat16)
    g_proj_w = jnp.einsum("rf,rd->fd", act, grad_mlp, preferred_element_type=jnp.float32)
    g_proj_b = column_sums(grad_mlp)
    grad_act = jnp.einsum("rd,fd->rf", grad_mlp, w_proj, preferred_element_type=jnp.float32)
    _, gelu_pull = jax.vjp(lambda value: jax.nn.gelu(value, approximate=True), pre)
    grad_pre = gelu_pull(grad_act)[0].astype(jnp.bfloat16)
    g_fc_w = jnp.einsum("rd,rf->df", normed2, grad_pre, preferred_element_type=jnp.float32)
    g_fc_b = column_sums(grad_pre)
    grad_n2 = jnp.einsum("rf,df->rd", grad_pre, w_fc, preferred_element_type=jnp.float32)
    g_ln2_g = jnp.sum(grad_n2 * hat2, axis=0)
    g_ln2_b = jnp.sum(grad_n2, axis=0)
    grad_mid = grad + norm_back(grad_n2 * ln2_g, hat2, inverse2)
    grad_branch = grad_mid.astype(jnp.bfloat16)
    g_out_w = jnp.einsum("rc,rd->cd", attended, grad_branch, preferred_element_type=jnp.float32)
    g_out_b = column_sums(grad_branch)
    grad_att = jnp.einsum(
        "rd,cd->rc", grad_branch, w_out, preferred_element_type=jnp.float32
    ).astype(jnp.bfloat16)
    block_lengths = jnp.repeat(lengths, 2)
    grad_q, grad_k, grad_v = lax.map(
        attend_back,
        (
            to_blocks(query, slots),
            to_blocks(keys, slots),
            to_blocks(values, slots),
            block_lengths,
            lse,
            to_blocks(grad_att, slots),
        ),
    )
    grad_q = from_blocks(grad_q, slots)
    grad_v = from_blocks(grad_v, slots)
    grad_qkv = jnp.concatenate([grad_q, from_blocks(grad_k, slots), grad_v], axis=1)
    g_qkv_w = jnp.einsum("rd,rc->dc", normed, grad_qkv, preferred_element_type=jnp.float32)
    g_qv_b = jnp.concatenate([column_sums(grad_q), column_sums(grad_v)])
    grad_n1 = jnp.einsum("rc,dc->rd", grad_qkv, w_qkv, preferred_element_type=jnp.float32)
    g_ln1_g = jnp.sum(grad_n1 * hat1, axis=0)
    g_ln1_b = jnp.sum(grad_n1, axis=0)
    grad_in = grad_mid + norm_back(grad_n1 * ln1_g, hat1, inverse1)
    grads = (
        g_ln1_g,
        g_ln1_b,
        g_qkv_w,
        g_qv_b,
        g_out_w,
        g_out_b,
        g_ln2_g,
        g_ln2_b,
        g_fc_w,
        g_fc_b,
        g_proj_w,
        g_proj_b,
    )
    return (grad_in, grads)


def pack_grads(grads, owners):
    return jnp.concatenate([member.reshape(owners, -1) for member in grads], axis=1)


def unpack_grads(flat, grads, owners):
    pieces = []
    offset = 0
    for member in grads:
        width = member.size // owners
        piece = flat[0, offset : offset + width]
        pieces.append(piece.reshape((member.shape[0] // owners,) + member.shape[1:]))
        offset = offset + width
    return tuple(pieces)


def body(
    tokens,
    cotangent,
    seq_len,
    ln1_gain,
    ln1_bias,
    qkv_weight,
    qv_bias,
    out_weight,
    out_bias,
    ln2_gain,
    ln2_bias,
    fc_weight,
    fc_bias,
    proj_weight,
    proj_bias,
):
    owners = lax.axis_size("dp")
    place = jnp.arange(SEQ, dtype=jnp.int32)
    live = (place[None, :] < seq_len[:, None]).reshape(-1, 1).astype(jnp.float32)
    state = tokens.astype(jnp.float32)
    kept_all = []
    fetched_all = []
    for index in range(LAYERS):
        weights = (
            lax.all_gather(ln1_gain[index], "dp", axis=0, tiled=True),
            lax.all_gather(ln1_bias[index], "dp", axis=0, tiled=True),
            lax.all_gather(qkv_weight[index], "dp", axis=0, tiled=True),
            lax.all_gather(qv_bias[index], "dp", axis=0, tiled=True),
            lax.all_gather(out_weight[index], "dp", axis=0, tiled=True),
            lax.all_gather(out_bias[index], "dp", axis=0, tiled=True),
            lax.all_gather(ln2_gain[index], "dp", axis=0, tiled=True),
            lax.all_gather(ln2_bias[index], "dp", axis=0, tiled=True),
            lax.all_gather(fc_weight[index], "dp", axis=0, tiled=True),
            lax.all_gather(fc_bias[index], "dp", axis=0, tiled=True),
            lax.all_gather(proj_weight[index], "dp", axis=0, tiled=True),
            lax.all_gather(proj_bias[index], "dp", axis=0, tiled=True),
        )
        state, kept = forward_layer(state, weights, seq_len)
        kept_all.append(kept)
        fetched_all.append(weights)
    output = (state * live).astype(jnp.bfloat16)
    grad = cotangent.astype(jnp.float32) * live
    layer_grads = [None] * LAYERS
    full_grads = [None] * LAYERS
    for index in reversed(range(LAYERS)):
        weights = (
            lax.all_gather(ln1_gain[index], "dp", axis=0, tiled=True),
            lax.all_gather(ln1_bias[index], "dp", axis=0, tiled=True),
            lax.all_gather(qkv_weight[index], "dp", axis=0, tiled=True),
            lax.all_gather(qv_bias[index], "dp", axis=0, tiled=True),
            lax.all_gather(out_weight[index], "dp", axis=0, tiled=True),
            lax.all_gather(out_bias[index], "dp", axis=0, tiled=True),
            lax.all_gather(ln2_gain[index], "dp", axis=0, tiled=True),
            lax.all_gather(ln2_bias[index], "dp", axis=0, tiled=True),
            lax.all_gather(fc_weight[index], "dp", axis=0, tiled=True),
            lax.all_gather(fc_bias[index], "dp", axis=0, tiled=True),
            lax.all_gather(proj_weight[index], "dp", axis=0, tiled=True),
            lax.all_gather(proj_bias[index], "dp", axis=0, tiled=True),
        )
        grad, grads = backward_layer(grad, weights, kept_all[index], seq_len)
        full_grads[index] = grads
        summed = lax.psum_scatter(pack_grads(grads, owners), "dp", scatter_dimension=0, tiled=True)
        layer_grads[index] = unpack_grads(summed, grads, owners)
    stacked = tuple(
        (jnp.stack([layer_grads[index][member] for index in range(LAYERS)]) for member in range(12))
    )
    return (
        output,
        grad.astype(jnp.bfloat16),
        stacked[0],
        stacked[1],
        stacked[2],
        stacked[3],
        stacked[4],
        stacked[5],
        stacked[6],
        stacked[7],
        stacked[8],
        stacked[9],
        stacked[10],
        stacked[11],
    )


def solution(mesh):
    placed = (
        P("dp", None),
        P("dp", None),
        P("dp"),
        P(None, "dp"),
        P(None, "dp"),
        P(None, "dp", None),
        P(None, "dp"),
        P(None, "dp", None),
        P(None, "dp"),
        P(None, "dp"),
        P(None, "dp"),
        P(None, "dp", None),
        P(None, "dp"),
        P(None, "dp", None),
        P(None, "dp"),
    )
    return jax.shard_map(
        body,
        mesh=mesh,
        in_specs=placed,
        out_specs=(
            P("dp", None),
            P("dp", None),
            P(None, "dp"),
            P(None, "dp"),
            P(None, "dp", None),
            P(None, "dp"),
            P(None, "dp", None),
            P(None, "dp"),
            P(None, "dp"),
            P(None, "dp"),
            P(None, "dp", None),
            P(None, "dp"),
            P(None, "dp", None),
            P(None, "dp"),
        ),
        check_vma=False,
    )
```

profile of v0, /device:TPU:0, one launch (start us, length us, event | category | flops | bytes accessed | tf_op | source)
XLA Modules:
  0.0 1861.1 jit_solution(1656482422500246251)
XLA Ops:
  26.0 43.7 %all-reduce.19 = (bf16[768]{0:T(1024)(128)(2,1)S(1)}, bf16[768]{0:T(1024)(128)(2,1)S(1)}, bf16[1536]{0:T(1024)(128)(2,1)S(1)}, bf16[768]{0:T(1024)(128)(2,1)S(1)...) all-reduce(bf16[768]{0:T(1024)(128)(2,1)S(1)} %dynamic-update-slice, ...), channel_id=3, replica_groups=mesh['dp'=32] {'dp'}, use_global_device_ids=true, to_apply=%add.1 | all-reduce | flops 18432 | bytes 73728
  83.5 15.5 while.52
  99.1 31.4 %all-gather.35.cloned.1.call-done = bf16[1,768,768]{2,1,0:T(8,128)(2,1)} async-done(((bf16[1,24,768]{2,1,0:T(8,128)(2,1)}), bf16[1,768,768]{2,1,0:T(8,128)(2,1)}) %all-gather.35.cloned.1.call-update) | async-done | bytes 1179664 | tf_op jit(solution)/shard_map/all_gather | solution.py:259
  134.4 62.2 %all-gather.37.cloned.1.call-done = bf16[1,768,3072]{2,1,0:T(8,128)(2,1)} async-done(((bf16[1,24,3072]{2,1,0:T(8,128)(2,1)}), bf16[1,768,3072]{2,1,0:T(8,128)(2,1)}) %all-gather.37.cloned.1.call-update) | async-done | bytes 4718608 | tf_op jit(solution)/shard_map/all_gather | solution.py:263
  196.6 8.3 fusion.162
  204.9 57.5 %all-gather.39.cloned.1.call-done = bf16[1,3072,768]{2,1,0:T(8,128)(2,1)} async-done(((bf16[1,96,768]{2,1,0:T(8,128)(2,1)}), bf16[1,3072,768]{2,1,0:T(8,128)(2,1)}) %all-gather.39.cloned.1.call-update) | async-done | bytes 4718608 | tf_op jit(solution)/shard_map/all_gather | solution.py:265
  262.4 8.6 fusion.239
  271.4 53.2 %all-gather.41.cloned.1.call-done = bf16[1,768,2304]{2,1,0:T(8,128)(2,1)} async-done(((bf16[1,24,2304]{2,1,0:T(8,128)(2,1)}), bf16[1,768,2304]{2,1,0:T(8,128)(2,1)}) %all-gather.41.cloned.1.call-update) | async-done | bytes 3538960 | tf_op jit(solution)/shard_map/all_gather | solution.py:257
  332.7 14.7 while.53
  347.4 32.8 %all-gather.43.cloned.1.call-done = bf16[1,768,768]{2,1,0:T(8,128)(2,1)} async-done(((bf16[1,24,768]{2,1,0:T(8,128)(2,1)}), bf16[1,768,768]{2,1,0:T(8,128)(2,1)}) %all-gather.43.cloned.1.call-update) | async-done | bytes 1179664 | tf_op jit(solution)/shard_map/all_gather | solution.py:259
  384.4 61.9 %all-gather.45.cloned.1.call-done = bf16[1,768,3072]{2,1,0:T(8,128)(2,1)} async-done(((bf16[1,24,3072]{2,1,0:T(8,128)(2,1)}), bf16[1,768,3072]{2,1,0:T(8,128)(2,1)}) %all-gather.45.cloned.1.call-update) | async-done | bytes 4718608 | tf_op jit(solution)/shard_map/all_gather | solution.py:263
  446.3 5.2 fusion.154
  454.2 6.2 fusion.225
  460.4 51.9 %all-gather.47.cloned.1.call-done = bf16[1,3072,768]{2,1,0:T(8,128)(2,1)} async-done(((bf16[1,96,768]{2,1,0:T(8,128)(2,1)}), bf16[1,3072,768]{2,1,0:T(8,128)(2,1)}) %all-gather.47.cloned.1.call-update) | async-done | bytes 4718608 | tf_op jit(solution)/shard_map/all_gather | solution.py:265
  512.3 9.8 convert_reduce_fusion
  522.1 5.7 fusion.231
  527.8 6.0 multiply_reduce_fusion.2
  542.3 86.1 %while.54 = (s32[]{:T(128)}, bf16[2,512,384]{1,2,0:T(8,128)(2,1)}, bf16[2,512,384]{1,2,0:T(8,128)(2,1)}, bf16[2,512,384]{1,2,0:T(8,128)(2,1)}, bf16[2,512,384]{1...) while((s32[]{:T(128)}, bf16[2,512,384]{1,2,0:T(8,128)(2,1)}, ...), condition=%wide.region_20.21_spmd, body=%wide.region_18.20_spmd.sunk | while | flops 1049042432 | bytes 54588576 | solution.py:178
  554.6 13.1 fusion.346
  573.9 10.6 fusion.348
  597.3 13.1 fusion.346
  616.7 10.6 fusion.348
  632.3 7.3 fusion.206
  644.1 6.3 fusion.219
  650.4 7.2 convert_reduce_fusion.1
  657.6 5.7 fusion.230
  675.2 84.4 %while.55 = (s32[]{:T(128)}, bf16[2,512,384]{1,2,0:T(8,128)(2,1)}, bf16[2,512,384]{1,2,0:T(8,128)(2,1)}, bf16[2,512,384]{1,2,0:T(8,128)(2,1)}, bf16[2,512,384]{1...) while((s32[]{:T(128)}, bf16[2,512,384]{1,2,0:T(8,128)(2,1)}, ...), condition=%wide.region_27.28_spmd, body=%wide.region_25.27_spmd.sunk | while | flops 1049042432 | bytes 54686908 | solution.py:178
  686.8 13.1 fusion.362
  706.1 10.5 fusion.364
  728.8 13.1 fusion.362
  748.1 10.5 fusion.364
  761.1 6.7 reshape.709
  770.0 8.1 reshape.714
  778.2 8.4 reshape.716
  787.2 5.2 fusion.205
  796.3 6.8 reshape.698
  805.2 8.1 reshape.703
  813.4 8.1 reshape.705
  827.3 20.5 %dynamic-update-slice.18 = f32[32,221472]{1,0:T(8,128)} dynamic-update-slice(f32[32,221472]{1,0:T(8,128)} %dynamic-update-slice.17, f32[32,55296]{1,0:T(8,128)} %reshape.709, s32[]{} %constant.233, s32[]{} %constant.235) | dynamic-update-slice | bytes 14155780
  847.9 20.7 %dynamic-update-slice.30 = f32[32,221472]{1,0:T(8,128)} dynamic-update-slice(f32[32,221472]{1,0:T(8,128)} %dynamic-update-slice.29, f32[32,55296]{1,0:T(8,128)} %reshape.698, s32[]{} %constant.233, s32[]{} %constant.235) | dynamic-update-slice | bytes 14155780
  871.5 8.9 dynamic-update-slice.20
  880.4 9.3 dynamic-update-slice.32
  898.7 28.8 %dynamic-update-slice.24 = f32[32,221472]{1,0:T(8,128)} dynamic-update-slice(f32[32,221472]{1,0:T(8,128)} %dynamic-update-slice.23, f32[32,73728]{1,0:T(8,128)} %reshape.714, s32[]{} %constant.233, s32[]{} %constant.242) | dynamic-update-slice | bytes 18874372
  927.5 28.8 %dynamic-update-slice.36 = f32[32,221472]{1,0:T(8,128)} dynamic-update-slice(f32[32,221472]{1,0:T(8,128)} %dynamic-update-slice.35, f32[32,73728]{1,0:T(8,128)} %reshape.703, s32[]{} %constant.233, s32[]{} %constant.242) | dynamic-update-slice | bytes 18874372
  959.3 28.3 %dynamic-update-slice.26 = f32[32,221472]{1,0:T(8,128)} dynamic-update-slice(f32[32,221472]{1,0:T(8,128)} %dynamic-update-slice.25, f32[32,73728]{1,0:T(8,128)} %reshape.716, s32[]{} %constant.233, s32[]{} %constant.244) | dynamic-update-slice | bytes 18874372
  987.6 28.3 %dynamic-update-slice.38 = f32[32,221472]{1,0:T(8,128)} dynamic-update-slice(f32[32,221472]{1,0:T(8,128)} %dynamic-update-slice.37, f32[32,73728]{1,0:T(8,128)} %reshape.705, s32[]{} %constant.233, s32[]{} %constant.244) | dynamic-update-slice | bytes 18874372
  1023.2 9.7 multiply_convert_fusion.2
  1032.9 793.2 %all-reduce.22.cloned.1.call-done = (f32[32,221472]{1,0:T(8,128)}, f32[32,221472]{1,0:T(8,128)}) async-done(((f32[32,221472]{1,0:T(8,128)}, f32[32,221472]{1,0:T(8,128)}), (f32[32,221472]{1,0:T(8,128)}, f32[32,221472]{1,0:T(8,128)})) %all-reduce.22.cloned.1.call-update) | async-done | bytes 56696848
  (499 shorter events, 249.7 us)
Async XLA Ops:
  7.2 69.2 %all-gather.33.cloned.1.call-start = ((), (), s32[]{:S(2)}) async-start(), calls=%async_computation | async-start | bytes 3649536 | tf_op jit(solution)/shard_map/all_gather | solution.py:257
  8.9 121.6 %all-gather.35.cloned.1.call-start = ((), (), s32[]{:S(2)}) async-start(), calls=%async_computation.1 | async-start | bytes 1216512 | tf_op jit(solution)/shard_map/all_gather | solution.py:259
  10.4 186.1 %all-gather.37.cloned.1.call-start = ((), (), s32[]{:S(2)}) async-start(), calls=%async_computation.2 | async-start | bytes 4866048 | tf_op jit(solution)/shard_map/all_gather | solution.py:263
  12.2 250.2 %all-gather.39.cloned.1.call-start = ((), (), s32[]{:S(2)}) async-start(), calls=%async_computation.3 | async-start | bytes 4866048 | tf_op jit(solution)/shard_map/all_gather | solution.py:265
  14.0 310.6 %all-gather.41.cloned.1.call-start = ((), (), s32[]{:S(2)}) async-start(), calls=%async_computation.4 | async-start | bytes 3649536 | tf_op jit(solution)/shard_map/all_gather | solution.py:257
  14.6 365.6 %all-gather.43.cloned.1.call-start = ((), (), s32[]{:S(2)}) async-start(), calls=%async_computation.5 | async-start | bytes 1216512 | tf_op jit(solution)/shard_map/all_gather | solution.py:259
  15.2 431.1 %all-gather.45.cloned.1.call-start = ((), (), s32[]{:S(2)}) async-start(), calls=%async_computation.6 | async-start | bytes 4866048 | tf_op jit(solution)/shard_map/all_gather | solution.py:263
  15.9 496.4 %all-gather.47.cloned.1.call-start = ((), (), s32[]{:S(2)}) async-start(), calls=%async_computation.7 | async-start | bytes 4866048 | tf_op jit(solution)/shard_map/all_gather | solution.py:265
  16.7 1809.5 %all-reduce.22.cloned.1.call-start = ((), (), s32[]{:S(2)}) async-start(), calls=%async_computation.8 | async-start | bytes 113442816
  70.3 10.5 copy-start.72
  70.3 10.5 copy-start.49
  71.6 9.2 copy-start.35
  73.8 122.7 %copy-start.74 = (f32[768]{0:T(1024)}, f32[768]{0:T(1024)S(1)}, u32[]{:S(2)}) copy-start(f32[768]{0:T(1024)S(1)} %convert_element_type.387) | copy-start | bytes 9220
  73.9 122.7 %copy-start.43 = (f32[768]{0:T(1024)}, f32[768]{0:T(1024)S(1)}, u32[]{:S(2)}) copy-start(f32[768]{0:T(1024)S(1)} %convert_element_type.386) | copy-start | bytes 9220
  73.9 188.5 %copy-start.58 = (f32[3072]{0:T(1024)}, f32[3072]{0:T(1024)S(1)}, u32[]{:S(2)}) copy-start(f32[3072]{0:T(1024)S(1)} %convert_element_type.388) | copy-start | bytes 36868
  73.9 250.7 %copy-start.76 = (f32[768]{0:T(1024)}, f32[768]{0:T(1024)S(1)}, u32[]{:S(2)}) copy-start(f32[768]{0:T(1024)S(1)} %convert_element_type.391) | copy-start | bytes 9220
  73.9 250.7 %copy-start.45 = (f32[768]{0:T(1024)}, f32[768]{0:T(1024)S(1)}, u32[]{:S(2)}) copy-start(f32[768]{0:T(1024)S(1)} %convert_element_type.390) | copy-start | bytes 9220
  83.5 47.0 %copy-start.13 = (bf16[512,768]{1,0:T(8,128)(2,1)S(1)}, bf16[512,768]{1,0:T(8,128)(2,1)}, u32[]{:S(2)}) copy-start(bf16[512,768]{1,0:T(8,128)(2,1)} %param.23) | copy-start | bytes 2359300
  99.0 105.8 %copy-start = (bf16[2,512,384]{1,2,0:T(8,128)(2,1)}, bf16[2,512,384]{1,2,0:T(8,128)(2,1)S(1)}, u32[]{:S(2)}) copy-start(bf16[2,512,384]{1,2,0:T(8,128)(2,1)S(1)} %get-tuple-element.754) | copy-start | bytes 2359300
  99.1 105.8 %copy-start.2 = (bf16[2,512,384]{1,2,0:T(8,128)(2,1)}, bf16[2,512,384]{1,2,0:T(8,128)(2,1)S(1)}, u32[]{:S(2)}) copy-start(bf16[2,512,384]{1,2,0:T(8,128)(2,1)S(1)} %get-tuple-element.755) | copy-start | bytes 2359300
  99.1 105.8 %copy-start.4 = (bf16[2,512,384]{1,2,0:T(8,128)(2,1)}, bf16[2,512,384]{1,2,0:T(8,128)(2,1)S(1)}, u32[]{:S(2)}) copy-start(bf16[2,512,384]{1,2,0:T(8,128)(2,1)S(1)} %get-tuple-element.756) | copy-start | bytes 2359300
  99.1 105.8 %copy-start.33 = (f32[2,6,512,1]{2,1,3,0:T(8,128)}, f32[2,6,512,1]{2,1,3,0:T(8,128)S(1)}, u32[]{:S(2)}) copy-start(f32[2,6,512,1]{2,1,3,0:T(8,128)S(1)} %get-tuple-element.713) | copy-start | bytes 73732
  132.9 71.9 %copy-start.37 = (f32[512]{0:T(512)}, f32[512]{0:T(512)S(1)}, u32[]{:S(2)}) copy-start(f32[512]{0:T(512)S(1)} %broadcast_multiply_fusion.10) | copy-start | bytes 6148
  134.4 70.5 %copy-start.64 = (f32[512]{0:T(512)}, f32[512]{0:T(512)S(1)}, u32[]{:S(2)}) copy-start(f32[512]{0:T(512)S(1)} %add_rsqrt_fusion.2) | copy-start | bytes 6148
  271.0 57.7 %copy-start.20 = (f32[512,768]{1,0:T(8,128)}, f32[512,768]{1,0:T(8,128)S(1)}, u32[]{:S(2)}) copy-start(f32[512,768]{1,0:T(8,128)S(1)} %get-tuple-element.380) | copy-start | bytes 4718596
  271.1 57.7 %copy-start.39 = (f32[512]{0:T(512)}, f32[512]{0:T(512)S(1)}, u32[]{:S(2)}) copy-start(f32[512]{0:T(512)S(1)} %broadcast_multiply_fusion.9) | copy-start | bytes 6148
  271.4 57.4 %copy-start.66 = (f32[512]{0:T(512)}, f32[512]{0:T(512)S(1)}, u32[]{:S(2)}) copy-start(f32[512]{0:T(512)S(1)} %add_rsqrt_fusion.1) | copy-start | bytes 6148
  332.7 47.5 %copy-start.77 = (f32[768]{0:T(1024)S(1)}, f32[768]{0:T(1024)}, u32[]{:S(2)}) copy-start(f32[768]{0:T(1024)} %convert_element_type.392) | copy-start | bytes 9220
  347.4 98.9 %copy-start.51 = (f32[768]{0:T(1024)S(1)}, f32[768]{0:T(1024)}, u32[]{:S(2)}) copy-start(f32[768]{0:T(1024)} %convert_element_type.393) | copy-start | bytes 9220
  347.4 98.9 %copy-start.78 = (f32[768]{0:T(1024)S(1)}, f32[768]{0:T(1024)}, u32[]{:S(2)}) copy-start(f32[768]{0:T(1024)} %convert_element_type.394) | copy-start | bytes 9220
  384.3 69.8 %copy-start.56 = (f32[3072]{0:T(1024)S(1)}, f32[3072]{0:T(1024)}, u32[]{:S(2)}) copy-start(f32[3072]{0:T(1024)} %convert_element_type.395) | copy-start | bytes 36868
  384.4 69.8 %copy-start.60 = (f32[512]{0:T(512)S(1)}, f32[512]{0:T(512)}, u32[]{:S(2)}) copy-start(f32[512]{0:T(512)} %fusion.211) | copy-start | bytes 6148
  512.3 9.8 copy-start.16
  632.2 11.8 slice-start.4
  644.1 19.2 %slice-start = ((s8[4718592]{0:T(1024)(128)(4,1)}), s8[4194304]{0:T(1024)(128)(4,1)S(1)}, s32[]{:S(2)}) async-start(s8[4718592]{0:T(1024)(128)(4,1)} %bitcast.415), calls=%async_computation.9 | async-start | bytes 8388608
  650.4 12.9 slice-start.1
  770.0 8.1 copy-start.54
  778.2 8.5 copy-start.47
  778.2 8.6 copy-start.23
  778.2 8.8 copy-start.22
  778.2 9.0 copy-start.14
  778.2 9.0 copy-start.29
  778.2 9.0 copy-start.36
  778.2 9.0 copy-start.50
  778.2 9.0 copy-start.63
  778.2 9.0 copy-start.73
  813.4 8.1 copy-start.41
  847.9 23.7 %copy-start.12 = (f32[32,18432]{1,0:T(8,128)S(1)}, f32[32,18432]{1,0:T(8,128)}, u32[]{:S(2)}) copy-start(f32[32,18432]{1,0:T(8,128)} %reshape.710) | copy-start | bytes 7077892
  (55 other events, 251.1 us)
Sparse Core Ops, SparseCore 0:
  11.5 63.1 all-gather.32
  77.5 52.8 all-gather.34
  134.0 62.5 all-gather.36
  199.9 62.4 all-gather.38
  265.7 58.8 all-gather.40
  327.4 52.8 all-gather.42
  383.7 62.5 all-gather.44
  449.8 62.4 all-gather.46
  1019.1 806.9 all-reduce.21
where the time goes:
time: 1870 us; the launch traced here: 1860 us
  waiting for transfers between devices  1150 us (61%)
  local copies, waits for them, and re-layouts  335 us (18%)
  matrix products  276 us (15%)
  blocking collectives  43.7 us (2%)
  other arithmetic  41.5 us (2%)
    unnamed x10, waiting for transfers between devices  796 us
    unnamed x240, local copies, waits for them, and re-layouts  210 us
    all_gather x2, waiting for transfers between devices, body(): lax.all_gather(fc_weight[index], 'dp', axis=0, tiled=True)  124 us
    all_gather x2, waiting for transfers between devices, body(): lax.all_gather(proj_weight[index], 'dp', axis=0, tiled=True)  109 us
    all_gather x2, waiting for transfers between devices, body(): lax.all_gather(out_weight[index], 'dp', axis=0, tiled=True)  64.2 us
    all_gather x2, waiting for transfers between devices, body(): lax.all_gather(qkv_weight[index], 'dp', axis=0, tiled=True)  53.2 us
    dot_general x4, matrix products, attend_back(): jnp.einsum('hqk,khd->qhd', grad_scores, k_heads, preferred_element_type=j...  52.6 us
    reshape x22, local copies, waits for them, and re-layouts, pack_grads(): member.reshape(owners, -1)  52 us
  transfers between devices with their start and end apart: 9, of which 8 were waited for; matrix products, arithmetic and copies ran while one was open for 6% of the time, Pallas kernels for 0%

commit v1 on v0

v1 whole, which is shorter than its diff:
```python
import math

import jax
import jax.numpy as jnp
from jax import lax
from jax.experimental import pallas as pl
from jax.experimental.pallas import tpu as pltpu
from jax.sharding import PartitionSpec as P

D = 768
HD = 64
SEQ = 512
LAYERS = 2


eps = 1e-05


def norm_stats(rows):
    mean = jnp.mean(rows, axis=-1, keepdims=True)
    centred = rows - mean
    var = jnp.mean(centred * centred, axis=-1, keepdims=True)
    inverse = lax.rsqrt(var + eps)
    return (centred * inverse, inverse)


def norm_back(grad_hat, hat, inverse):
    first = jnp.mean(grad_hat, axis=-1, keepdims=True)
    second = jnp.mean(grad_hat * hat, axis=-1, keepdims=True)
    return inverse * (grad_hat - first - hat * second)


def block_probs(query, keys, allowed):
    scores = lax.dot_general(
        query, keys, (((1,), (1,)), ((), ())), preferred_element_type=jnp.float32
    ) * (1.0 / math.sqrt(HD))
    scores = jnp.where(allowed, scores, -1e30)
    top = jnp.max(scores, axis=-1, keepdims=True)
    expo = jnp.exp(scores - top)
    return expo * (1.0 / jnp.sum(expo, axis=-1, keepdims=True))


def block_allowed(first, count, seen, length):
    row = lax.broadcasted_iota(jnp.int32, (count, seen), 0) + first
    column = lax.broadcasted_iota(jnp.int32, (count, seen), 1)
    return (column <= row) & (column < length)


def attend_kernel(length_ref, query_ref, keys_ref, values_ref, out_ref):
    length = length_ref[pl.program_id(0)]
    half = SEQ // 2
    for part in range(2):
        first, seen = part * half, (part + 1) * half
        rows = pl.ds(first, half)
        allowed = block_allowed(first, half, seen, length)
        for head in range(128 // HD):
            lanes = pl.ds(head * HD, HD)
            probs = block_probs(query_ref[rows, lanes], keys_ref[pl.ds(0, seen), lanes], allowed)
            attended = jnp.dot(
                probs.astype(jnp.bfloat16),
                values_ref[pl.ds(0, seen), lanes],
                preferred_element_type=jnp.float32,
            )
            out_ref[rows, lanes] = attended.astype(jnp.bfloat16)


def attend_back_kernel(
    length_ref, query_ref, keys_ref, values_ref, grad_ref, dq_ref, dk_ref, dv_ref
):
    length = length_ref[pl.program_id(0)]
    half = SEQ // 2
    scale = 1.0 / math.sqrt(HD)
    over_rows = (((0,), (0,)), ((), ()))
    for head in range(128 // HD):
        lanes = pl.ds(head * HD, HD)
        sums = []
        for part in range(2):
            first, seen = part * half, (part + 1) * half
            rows = pl.ds(first, half)
            keys = keys_ref[pl.ds(0, seen), lanes]
            query = query_ref[rows, lanes]
            grad = grad_ref[rows, lanes]
            allowed = block_allowed(first, half, seen, length)
            probs = block_probs(query, keys, allowed)
            dprob = lax.dot_general(
                grad,
                values_ref[pl.ds(0, seen), lanes],
                (((1,), (1,)), ((), ())),
                preferred_element_type=jnp.float32,
            )
            delta = jnp.sum(probs * dprob, axis=-1, keepdims=True)
            dscores = (probs * (dprob - delta)).astype(jnp.bfloat16)
            dq = jnp.dot(dscores, keys, preferred_element_type=jnp.float32) * scale
            dq_ref[rows, lanes] = dq.astype(jnp.bfloat16)
            dk = lax.dot_general(dscores, query, over_rows, preferred_element_type=jnp.float32)
            dv = lax.dot_general(
                probs.astype(jnp.bfloat16), grad, over_rows, preferred_element_type=jnp.float32
            )
            sums.append((dk, dv))
        low, high = pl.ds(0, half), pl.ds(half, half)
        (dk0, dv0), (dk1, dv1) = sums
        dk_ref[low, lanes] = ((dk0 + dk1[:half]) * scale).astype(jnp.bfloat16)
        dk_ref[high, lanes] = (dk1[half:] * scale).astype(jnp.bfloat16)
        dv_ref[low, lanes] = (dv0 + dv1[:half]).astype(jnp.bfloat16)
        dv_ref[high, lanes] = dv1[half:].astype(jnp.bfloat16)


def pair_block(offset):
    return pl.BlockSpec((SEQ, 128), lambda slot, pair: (slot, pair + offset))


def attend(qkv, lengths):
    pairs = D // 128
    return pl.pallas_call(
        attend_kernel,
        grid=(lengths.shape[0], pairs),
        in_specs=[pl.BlockSpec(memory_space=pltpu.SMEM)]
        + [pair_block(pairs * kind) for kind in range(3)],
        out_specs=pair_block(0),
        out_shape=jax.ShapeDtypeStruct((qkv.shape[0], D), jnp.bfloat16),
        compiler_params=pltpu.CompilerParams(vmem_limit_bytes=48 * 2**20),
        name="attend",
    )(lengths, qkv, qkv, qkv)


def attend_back(qkv, grad_att, lengths):
    pairs = D // 128
    shape = jax.ShapeDtypeStruct((qkv.shape[0], D), jnp.bfloat16)
    return pl.pallas_call(
        attend_back_kernel,
        grid=(lengths.shape[0], pairs),
        in_specs=[pl.BlockSpec(memory_space=pltpu.SMEM)]
        + [pair_block(pairs * kind) for kind in range(3)]
        + [pair_block(0)],
        out_specs=[pair_block(0)] * 3,
        out_shape=[shape] * 3,
        compiler_params=pltpu.CompilerParams(vmem_limit_bytes=48 * 2**20),
        name="attend_back",
    )(lengths, qkv, qkv, qkv, grad_att)


def forward_layer(state, weights, lengths):
    ln1_g, ln1_b, w_qkv, b_qv, w_out, b_out, ln2_g, ln2_b, w_fc, b_fc, w_proj, b_proj = weights
    hat1, inverse1 = norm_stats(state)
    normed = (hat1 * ln1_g + ln1_b).astype(jnp.bfloat16)
    qkv = jnp.dot(normed, w_qkv, preferred_element_type=jnp.float32)
    zeros = jnp.zeros((D,), b_qv.dtype)
    qkv = (qkv + jnp.concatenate([b_qv[:D], zeros, b_qv[D:]])).astype(jnp.bfloat16)
    attended = attend(qkv, lengths)
    middle = state + jnp.dot(attended, w_out, preferred_element_type=jnp.float32) + b_out
    hat2, inverse2 = norm_stats(middle)
    normed2 = (hat2 * ln2_g + ln2_b).astype(jnp.bfloat16)
    pre = jnp.dot(normed2, w_fc, preferred_element_type=jnp.float32) + b_fc
    act = jax.nn.gelu(pre, approximate=True).astype(jnp.bfloat16)
    result = middle + jnp.dot(act, w_proj, preferred_element_type=jnp.float32) + b_proj
    kept = (
        hat1,
        inverse1,
        normed,
        qkv,
        attended,
        hat2,
        inverse2,
        normed2,
        pre,
        act,
    )
    return (result, kept)


def column_sums(matrix):
    return jnp.sum(matrix.astype(jnp.float32), axis=0)


def backward_layer(grad, weights, kept, lengths):
    ln1_g, ln1_b, w_qkv, b_qv, w_out, b_out, ln2_g, ln2_b, w_fc, b_fc, w_proj, b_proj = weights
    (
        hat1,
        inverse1,
        normed,
        qkv,
        attended,
        hat2,
        inverse2,
        normed2,
        pre,
        act,
    ) = kept
    grad_mlp = grad.astype(jnp.bfloat16)
    g_proj_w = jnp.einsum("rf,rd->fd", act, grad_mlp, preferred_element_type=jnp.float32)
    g_proj_b = column_sums(grad_mlp)
    grad_act = jnp.einsum("rd,fd->rf", grad_mlp, w_proj, preferred_element_type=jnp.float32)
    _, gelu_pull = jax.vjp(lambda value: jax.nn.gelu(value, approximate=True), pre)
    grad_pre = gelu_pull(grad_act)[0].astype(jnp.bfloat16)
    g_fc_w = jnp.einsum("rd,rf->df", normed2, grad_pre, preferred_element_type=jnp.float32)
    g_fc_b = column_sums(grad_pre)
    grad_n2 = jnp.einsum("rf,df->rd", grad_pre, w_fc, preferred_element_type=jnp.float32)
    g_ln2_g = jnp.sum(grad_n2 * hat2, axis=0)
    g_ln2_b = jnp.sum(grad_n2, axis=0)
    grad_mid = grad + norm_back(grad_n2 * ln2_g, hat2, inverse2)
    grad_branch = grad_mid.astype(jnp.bfloat16)
    g_out_w = jnp.einsum("rc,rd->cd", attended, grad_branch, preferred_element_type=jnp.float32)
    g_out_b = column_sums(grad_branch)
    grad_att = jnp.einsum(
        "rd,cd->rc", grad_branch, w_out, preferred_element_type=jnp.float32
    ).astype(jnp.bfloat16)
    grad_q, grad_k, grad_v = attend_back(qkv, grad_att, lengths)
    grad_qkv = jnp.concatenate([grad_q, grad_k, grad_v], axis=1)
    g_qkv_w = jnp.einsum("rd,rc->dc", normed, grad_qkv, preferred_element_type=jnp.float32)
    g_qv_b = jnp.concatenate([column_sums(grad_q), column_sums(grad_v)])
    grad_n1 = jnp.einsum("rc,dc->rd", grad_qkv, w_qkv, preferred_element_type=jnp.float32)
    g_ln1_g = jnp.sum(grad_n1 * hat1, axis=0)
    g_ln1_b = jnp.sum(grad_n1, axis=0)
    grad_in = grad_mid + norm_back(grad_n1 * ln1_g, hat1, inverse1)
    grads = (
        g_ln1_g,
        g_ln1_b,
        g_qkv_w,
        g_qv_b,
        g_out_w,
        g_out_b,
        g_ln2_g,
        g_ln2_b,
        g_fc_w,
        g_fc_b,
        g_proj_w,
        g_proj_b,
    )
    return (grad_in, grads)


WIDTHS = (1, 1, 3 * D, 2, D, 1, 1, 1, 4 * D, 4, 4 * D, 1)


def pack(members, rows):
    wide = [member.reshape(rows, -1).astype(jnp.bfloat16) for member in members]
    large = [member for member in wide if member.shape[1] >= 128]
    small = jnp.concatenate([member for member in wide if member.shape[1] < 128], axis=1)
    small = jnp.pad(small, ((0, 0), (0, 128 - small.shape[1])))
    return jnp.concatenate(large + [small], axis=1)


def unpack(packed):
    large, small = 0, sum(width for width in WIDTHS if width >= 128)
    pieces = []
    for width in WIDTHS:
        if width >= 128:
            pieces.append(packed[:, large : large + width])
            large = large + width
        else:
            pieces.append(packed[:, small : small + width])
            small = small + width
    return pieces


def fetch(members):
    rows = members[0].shape[0]
    whole = lax.all_gather(pack(members, rows), "dp", axis=0, tiled=True)
    shapes = [(-1,) + member.shape[1:] for member in members]
    return tuple(piece.reshape(shape) for piece, shape in zip(unpack(whole), shapes))


def reduce_to_owners(grads, earlier):
    packed = pack(grads, D)
    if earlier is not None:
        packed, earlier = lax.optimization_barrier((packed, earlier))
    return lax.psum_scatter(packed, "dp", scatter_dimension=0, tiled=True), earlier


def shares_of(mine, shards):
    return [
        piece.astype(jnp.float32).reshape(shard.shape)
        for piece, shard in zip(unpack(mine), shards)
    ]


def body(tokens, cotangent, seq_len, *params):
    place = jnp.arange(SEQ, dtype=jnp.int32)
    live = (place[None, :] < seq_len[:, None]).reshape(-1, 1).astype(jnp.float32)
    shards = [tuple(member[index] for member in params) for index in range(LAYERS)]
    weights = [fetch(members) for members in shards]
    state = tokens.astype(jnp.float32)
    kept_all = []
    for index in range(LAYERS):
        state, kept = forward_layer(state, weights[index], seq_len)
        kept_all.append(kept)
    output = (state * live).astype(jnp.bfloat16)
    grad = cotangent.astype(jnp.float32) * live
    mine = [None] * (LAYERS + 1)
    for index in reversed(range(LAYERS)):
        grad, grads = backward_layer(grad, weights[index], kept_all[index], seq_len)
        mine[index], mine[index + 1] = reduce_to_owners(grads, mine[index + 1])
    layer_grads = [shares_of(mine[index], shards[index]) for index in range(LAYERS)]
    stacked = tuple(
        jnp.stack([layer_grads[index][member] for index in range(LAYERS)]) for member in range(12)
    )
    return (output, grad.astype(jnp.bfloat16)) + stacked


def solution(mesh):
    placed = (
        P("dp", None),
        P("dp", None),
        P("dp"),
        P(None, "dp"),
        P(None, "dp"),
        P(None, "dp", None),
        P(None, "dp"),
        P(None, "dp", None),
        P(None, "dp"),
        P(None, "dp"),
        P(None, "dp"),
        P(None, "dp", None),
        P(None, "dp"),
        P(None, "dp", None),
        P(None, "dp"),
    )
    return jax.shard_map(
        body,
        mesh=mesh,
        in_specs=placed,
        out_specs=(
            P("dp", None),
            P("dp", None),
            P(None, "dp"),
            P(None, "dp"),
            P(None, "dp", None),
            P(None, "dp"),
            P(None, "dp", None),
            P(None, "dp"),
            P(None, "dp"),
            P(None, "dp"),
            P(None, "dp", None),
            P(None, "dp"),
            P(None, "dp", None),
            P(None, "dp"),
        ),
        check_vma=False,
    )
```

time: 1870 us -> 869 us (0.46)
  waiting for transfers between devices: 1150 us -> 513 us
  local copies, waits for them, and re-layouts: 335 us -> 107 us
  matrix products: 276 us -> 134 us
  Pallas kernels: 0 us -> 59.9 us
  blocking collectives: 43.7 us -> 0 us
    unnamed x10 -> x5, waiting for transfers between devices: 796 us -> 243 us
    unnamed x240 -> x185, local copies, waits for them, and re-layouts: 210 us -> 21.9 us
    dot_general x28 -> x0, matrix products: 154 us -> none  [the longest x4 52.6 us: attend_back(): jnp.einsum('hqk,khd->qhd', grad_scores, k_heads, preferred_element_type=j...]
    all_gather x8 -> x2, waiting for transfers between devices: 351 us -> 208 us  [fetch(): whole = lax.all_gather(pack(members, rows), 'dp', axis=0, tiled=True)]
    optimization_barrier x0 -> x1, waiting for transfers between devices: none -> 61.8 us  [reduce_to_owners(): packed, earlier = lax.optimization_barrier((packed, earlier))]
    pallas_call x0 -> x4, Pallas kernels: none -> 59.9 us  [the longest x2 35.5 us: attend_back(): pl.pallas_call(attend_back_kernel, grid=(lengths.shape[0], pairs), in_spe...]
    unnamed x1 -> x0, blocking collectives: 43.7 us -> none
    reshape x31 -> x2, local copies, waits for them, and re-layouts: 57.8 us -> 16.9 us  [fetch(): piece.reshape(shape)]
  transfers between devices with their start and end apart: 9 -> 4, of which waited for: 8 -> 4; matrix products, arithmetic and copies ran while one was open for 6% -> 11% of each run, Pallas kernels for 0% -> 2%
where the time goes in v1:
time: 869 us; the launch traced here: 862 us
  waiting for transfers between devices  513 us (59%)
  matrix products  134 us (15%)
  local copies, waits for them, and re-layouts  107 us (12%)
  Pallas kernels  59.9 us (7%)
  other arithmetic  31.7 us (4%)
  between operations  16.3 us (2%)
    unnamed x5, waiting for transfers between devices  243 us
    all_gather x2, waiting for transfers between devices, fetch(): whole = lax.all_gather(pack(members, rows), 'dp', axis=0, tiled=True)  208 us
    optimization_barrier x1, waiting for transfers between devices, reduce_to_owners(): packed, earlier = lax.optimization_barrier((packed, earlier))  61.8 us
    pallas_call x2, Pallas kernels, attend_back(): pl.pallas_call(attend_back_kernel, grid=(lengths.shape[0], pairs), in_spe...  35.5 us
    convert_element_type x18, local copies, waits for them, and re-layouts, pack(): wide = [member.reshape(rows, -1).astype(jnp.bfloat16) for member in members]  31.2 us
    pallas_call x2, Pallas kernels, attend(): pl.pallas_call(attend_kernel, grid=(lengths.shape[0], pairs), in_specs=[p...  24.5 us
    unnamed x185, local copies, waits for them, and re-layouts  21.9 us
    dot_general x2, matrix products, backward_layer(): jnp.einsum('rd,fd->rf', grad_mlp, w_proj, preferred_element_type=jnp.floa...  19.4 us
  transfers between devices with their start and end apart: 4, of which 4 were waited for; matrix products, arithmetic and copies ran while one was open for 11% of the time, Pallas kernels for 2%

profile of v1, /device:TPU:0, one launch (start us, length us, event | category | flops | bytes accessed | tf_op | source)
XLA Modules:
  0.0 862.5 jit_solution(8259366451543725122)
XLA Ops:
  22.0 103.8 %all-gather.5.cloned.1.call-done = bf16[768,9344]{1,0:T(8,128)(2,1)} async-done(((bf16[24,9344]{1,0:T(8,128)(2,1)}), bf16[768,9344]{1,0:T(8,128)(2,1)}) %all-gather.5.cloned.1.call-update) | async-done | bytes 14352400 | tf_op jit(solution)/shard_map/all_gather | solution.py:258
  127.1 104.4 %all-gather.3.cloned.1.call-done = bf16[768,9344]{1,0:T(8,128)(2,1)} async-done(((bf16[24,9344]{1,0:T(8,128)(2,1)}), bf16[768,9344]{1,0:T(8,128)(2,1)}) %all-gather.3.cloned.1.call-update) | async-done | bytes 14352400 | tf_op jit(solution)/shard_map/all_gather | solution.py:258
  235.5 2.3 convert_reduce_fusion.9
  237.8 4.2 fusion.18.query_ref.keys_ref.values_ref
  242.0 12.2 %attend.2 = bf16[512,768]{1,0:T(8,128)(2,1)S(1)} custom-call(s32[1]{0:T(128)} %copy.170.length_ref, bf16[512,2304]{1,0:T(8,128)(2,1)S(1)} %fusion.18.query_ref.keys_ref.values_ref, bf16[512,2304]{1,0:T(8,128)(2,1)S(1)} %fusion.18.query_ref.keys_ref.values_ref, bf16[512,2304]{1,0:T(8,128)(2,1)S(1)} %fusion.18.query_ref.keys_ref.values_ref), custom_call_target="tpu_custom_call" | custom-call | tf_op jit(solution)/shard_map/attend/pallas_call | solution.py:114
  254.3 2.1 fusion.86
  257.9 4.8 slice.317
  262.7 8.5 reshape.426
  271.2 4.8 slice.330
  275.9 8.5 reshape.427
  284.4 5.3 fusion.26
  289.7 8.6 fusion.87
  298.7 3.0 convert_reduce_fusion.3
  301.7 4.1 fusion.19.query_ref.keys_ref.values_ref
  305.9 12.3 %attend.3 = bf16[512,768]{1,0:T(8,128)(2,1)S(1)} custom-call(s32[1]{0:T(128)} %copy.170.length_ref, bf16[512,2304]{1,0:T(8,128)(2,1)S(1)} %fusion.19.query_ref.keys_ref.values_ref, bf16[512,2304]{1,0:T(8,128)(2,1)S(1)} %fusion.19.query_ref.keys_ref.values_ref, bf16[512,2304]{1,0:T(8,128)(2,1)S(1)} %fusion.19.query_ref.keys_ref.values_ref), custom_call_target="tpu_custom_call" | custom-call | tf_op jit(solution)/shard_map/attend/pallas_call | solution.py:114
  318.2 2.4 fusion.88
  321.0 4.9 fusion.22
  326.0 5.5 convolution_convert_fusion
  331.5 8.3 fusion.90
  339.8 8.9 %convert_element_type.547 = bf16[768,3072]{1,0:T(8,128)(2,1)} reshape(bf16[3072,768]{1,0:T(8,128)(2,1)} %convolution_convert_fusion) | data formatting | bytes 9437184 | tf_op jit(solution)/shard_map/convert_element_type | solution.py:236
  349.1 6.9 multiply_reduce_fusion
  361.7 2.4 copy.148
  364.0 2.7 convolution_convert_fusion.9.grad_ref
  366.8 17.7 %attend_back.2 = (bf16[512,768]{1,0:T(8,128)(2,1)S(1)}, bf16[512,768]{1,0:T(8,128)(2,1)S(1)}, bf16[512,768]{1,0:T(8,128)(2,1)S(1)}) custom-call(s32[1]{0:T(128)} %copy.170.length_ref, bf16[512,2304]{1,0:T(8,128)(2,1)S(1)} %copy-done.1, bf16[512,2304]{1,0:T(8,128)(2,1)S(1)} %copy-done.1, bf16[512,2304]{1,0:T(8,128)(2,1)S(1)} %copy-done.1, ...), custom_call_target="tpu_custom_call" | custom-call | tf_op jit(solution)/shard_map/attend_back/pallas_call | solution.py:129
  389.4 2.1 constant_dynamic-update-slice_fusion.7
  391.5 2.7 fusion.81
  395.8 6.3 fusion.17
  402.2 6.1 multiply_reduce_fusion.1
  411.2 4.8 fusion.14
  416.8 2.5 constant_dynamic-update-slice_fusion.14
  419.3 2.4 concatenate.93
  424.0 3.5 convert_reduce_fusion.14
  428.7 9.1 %convolution_convert_fusion.3 = bf16[3072,768]{1,0:T(8,128)(2,1)} fusion(f32[512,768]{1,0:T(8,128)S(1)} %get-tuple-element.77, f32[512,3072]{1,0:T(8,128)} %copy-done.78, f32[3072]{0:T(1024)S(1)} %copy-done.50), kind=kOutput, calls=%fused_computation.24 | convolution fusion | flops 2434400256 | bytes 12595200 | tf_op jit(solution)/shard_map/rf,rd->fd/dot_general | solution.py:190
  437.8 8.9 %convert_element_type.529 = bf16[768,3072]{1,0:T(8,128)(2,1)} reshape(bf16[3072,768]{1,0:T(8,128)(2,1)} %convolution_convert_fusion.3) | data formatting | bytes 9437184 | tf_op jit(solution)/shard_map/convert_element_type | solution.py:236
  446.7 11.1 %fusion.89 = (bf16[3072]{0:T(1024)(128)(2,1)S(1)}, bf16[512,3072]{1,0:T(8,128)(2,1)}) fusion(f32[512,3072]{1,0:T(8,128)} %copy-done.78, f32[3072]{0:T(1024)S(1)} %copy-done.50, bf16[3072,768]{1,0:T(8,128)(2,1)} %reshape.426, f32[512,768]{1,0:T(8,128)} %copy-done.23), kind=kOutput, calls=%fused_computation.234 | convolution fusion | flops 2450912256 | bytes 15747072 | tf_op jit(solution)/shard_map/rd,fd->rf/dot_general | solution.py:192
  458.5 7.7 multiply_reduce_fusion.2
  471.4 2.4 copy.141
  473.8 3.0 convolution_convert_fusion.8.grad_ref
  476.8 17.8 %attend_back.3 = (bf16[512,768]{1,0:T(8,128)(2,1)S(1)}, bf16[512,768]{1,0:T(8,128)(2,1)S(1)}, bf16[512,768]{1,0:T(8,128)(2,1)S(1)}) custom-call(s32[1]{0:T(128)} %copy.170.length_ref, bf16[512,2304]{1,0:T(8,128)(2,1)S(1)} %fusion.18.query_ref.keys_ref.values_ref, bf16[512,2304]{1,0:T(8,128)(2,1)S(1)} %fusion.18.query_ref.keys_ref.values_ref, ...), custom_call_target="tpu_custom_call" | custom-call | tf_op jit(solution)/shard_map/attend_back/pallas_call | solution.py:129
  496.8 2.2 constant_dynamic-update-slice_fusion.10
  500.2 6.7 fusion.47
  508.2 5.8 fusion.16
  515.2 5.1 fusion.15
  520.4 2.5 constant_dynamic-update-slice_fusion.12
  523.6 61.8 %reduce-scatter.4.cloned.1.call-done = bf16[24,9344]{1,0:T(8,128)(2,1)} async-done(((bf16[768,9344]{1,0:T(8,128)(2,1)}), bf16[24,9344]{1,0:T(8,128)(2,1)}) %reduce-scatter.4.cloned.1.call-update) | async-done | bytes 448528 | tf_op jit(solution)/shard_map/optimization_barrier | solution.py:266
  585.6 3.0 fusion.46
  588.6 9.0 %multiply_convert_fusion.2 = bf16[512,768]{1,0:T(8,128)(2,1)} fusion(f32[512,768]{1,0:T(8,128)S(1)} %copy-done.16, bf16[3072,768]{1,0:T(8,128)(2,1)} %reshape.427, f32[512]{0:T(512)S(1)} %copy-done.53, f32[768]{0:T(1024)S(1)} %copy-done.65, f32[512,3072]{1,0:T(8,128)} %copy-done.77, f32[3072]{0:T(1024)S(1)} %copy-done.48), kind=kOutput, calls=%fused_computation.78 | convolution fusion | flops 2433220608 | bytes 13386752 | tf_op jit(solution)/shard_map/dot_general | solution.py:155
  598.4 243.3 %all-reduce.8.cloned.1.call-done = bf16[768,9344]{1,0:T(8,128)(2,1)} async-done(((bf16[768,9344]{1,0:T(8,128)(2,1)}), bf16[768,9344]{1,0:T(8,128)(2,1)}) %all-reduce.8.cloned.1.call-update) | async-done | bytes 14352400
  (316 shorter events, 67.9 us)
Async XLA Ops:
  7.2 14.2 %copy-start.10 = (bf16[512,768]{1,0:T(8,128)(2,1)S(1)}, bf16[512,768]{1,0:T(8,128)(2,1)}, u32[]{:S(2)}) copy-start(bf16[512,768]{1,0:T(8,128)(2,1)} %param.15) | copy-start | bytes 2359300
  7.2 118.6 %all-gather.5.cloned.1.call-start = ((), (), s32[]{:S(2)}) async-start(), calls=%async_computation.2 | async-start | bytes 14800896 | tf_op jit(solution)/shard_map/all_gather | solution.py:258
  18.8 212.7 %all-gather.3.cloned.1.call-start = ((), (), s32[]{:S(2)}) async-start(), calls=%async_computation.1 | async-start | bytes 14800896 | tf_op jit(solution)/shard_map/all_gather | solution.py:258
  20.7 564.8 %reduce-scatter.4.cloned.1.call-start = ((), (), s32[]{:S(2)}) async-start(), calls=%async_computation.4 | async-start | bytes 14800896
  21.4 334.6 %copy-start.52 = (f32[512]{0:T(512)}, f32[512]{0:T(512)S(1)}, u32[]{:S(2)}) copy-start(f32[512]{0:T(512)S(1)} %fusion.59) | copy-start | bytes 6148
  22.0 220.0 %copy-start.62 = (f32[512]{0:T(512)}, f32[512]{0:T(512)S(1)}, u32[]{:S(2)}) copy-start(f32[512]{0:T(512)S(1)} %add_rsqrt_fusion.3) | copy-start | bytes 6148
  234.2 55.5 %copy-start.49 = (f32[3072]{0:T(1024)}, f32[3072]{0:T(1024)S(1)}, u32[]{:S(2)}) copy-start(f32[3072]{0:T(1024)S(1)} %reshape.433) | copy-start | bytes 36868
  235.4 96.0 %copy-start.47 = (f32[3072]{0:T(1024)}, f32[3072]{0:T(1024)S(1)}, u32[]{:S(2)}) copy-start(f32[3072]{0:T(1024)S(1)} %reshape.440) | copy-start | bytes 36868
  237.8 46.6 %copy-start.38 = (f32[768]{0:T(1024)}, f32[768]{0:T(1024)S(1)}, u32[]{:S(2)}) copy-start(f32[768]{0:T(1024)S(1)} %get-tuple-element.42) | copy-start | bytes 9220
  237.8 46.6 %copy-start.66 = (f32[768]{0:T(1024)}, f32[768]{0:T(1024)S(1)}, u32[]{:S(2)}) copy-start(f32[768]{0:T(1024)S(1)} %get-tuple-element.44) | copy-start | bytes 9220
  242.0 12.2 %copy-start.11 = (bf16[512,768]{1,0:T(8,128)(2,1)S(1)}, bf16[512,768]{1,0:T(8,128)(2,1)}, u32[]{:S(2)}) copy-start(bf16[512,768]{1,0:T(8,128)(2,1)} %param.15) | copy-start | bytes 2359300
  257.9 26.5 %copy-start.54 = (f32[512]{0:T(512)}, f32[512]{0:T(512)S(1)}, u32[]{:S(2)}) copy-start(f32[512]{0:T(512)S(1)} %add_rsqrt_fusion.2) | copy-start | bytes 6148
  289.7 8.7 %copy-start.78 = (f32[512,3072]{1,0:T(8,128)}, f32[512,3072]{1,0:T(8,128)S(1)}, u32[]{:S(2)}) copy-start(f32[512,3072]{1,0:T(8,128)S(1)} %fusion.26) | copy-start | bytes 18874372
  298.4 19.8 %copy-start.21 = (f32[512,768]{1,0:T(8,128)}, f32[512,768]{1,0:T(8,128)S(1)}, u32[]{:S(2)}) copy-start(f32[512,768]{1,0:T(8,128)S(1)} %get-tuple-element.122) | copy-start | bytes 4718596
  298.7 7.2 copy-start.57
  301.7 19.2 %copy-start.70 = (f32[768]{0:T(1024)}, f32[768]{0:T(1024)S(1)}, u32[]{:S(2)}) copy-start(f32[768]{0:T(1024)S(1)} %get-tuple-element.38) | copy-start | bytes 9220
  301.7 54.3 %copy-start.43 = (f32[768]{0:T(1024)}, f32[768]{0:T(1024)S(1)}, u32[]{:S(2)}) copy-start(f32[768]{0:T(1024)S(1)} %get-tuple-element.36) | copy-start | bytes 9220
  305.9 12.3 %copy-start = (bf16[512,2304]{1,0:T(8,128)(2,1)}, bf16[512,2304]{1,0:T(8,128)(2,1)S(1)}, u32[]{:S(2)}) copy-start(bf16[512,2304]{1,0:T(8,128)(2,1)S(1)} %fusion.19.query_ref.keys_ref.values_ref) | copy-start | bytes 7077892
  321.0 35.1 %copy-start.60 = (f32[512]{0:T(512)}, f32[512]{0:T(512)S(1)}, u32[]{:S(2)}) copy-start(f32[512]{0:T(512)S(1)} %add_rsqrt_fusion) | copy-start | bytes 6148
  321.0 10.4 %slice-start.4 = ((s8[4718592]{0:T(1024)(128)(4,1)}), s8[4194304]{0:T(1024)(128)(4,1)S(1)}, s32[]{:S(2)}) async-start(s8[4718592]{0:T(1024)(128)(4,1)} %bitcast.82), calls=%async_computation.9 | async-start | bytes 8388608
  349.1 6.9 copy-start.14
  349.1 6.9 copy-start.28
  395.8 6.3 copy-start.22
  395.8 6.3 copy-start.37
  395.8 6.3 copy-start.41
  395.8 6.3 copy-start.58
  402.2 7.8 copy-start.26
  402.2 9.0 %copy-start.80 = (bf16[512,3072]{1,0:T(8,128)(2,1)S(1)}, bf16[512,3072]{1,0:T(8,128)(2,1)}, u32[]{:S(2)}) copy-start(bf16[512,3072]{1,0:T(8,128)(2,1)} %get-tuple-element.132) | copy-start | bytes 9437188
  410.0 6.8 slice-start.2
  423.3 418.4 %all-reduce.8.cloned.1.call-start = ((), (), s32[]{:S(2)}) async-start(), calls=%async_computation.3 | async-start | bytes 28704768
  446.7 11.6 %copy-start.51 = (bf16[768]{0:T(1024)(128)(2,1)S(1)}, bf16[768]{0:T(1024)(128)(2,1)}, u32[]{:S(2)}) copy-start(bf16[768]{0:T(1024)(128)(2,1)} %get-tuple-element.76) | copy-start | bytes 4612
  446.7 11.7 %copy-start.39 = (f32[768]{0:T(1024)S(1)}, f32[768]{0:T(1024)}, u32[]{:S(2)}) copy-start(f32[768]{0:T(1024)} %copy-done.38) | copy-start | bytes 9220
  458.4 7.8 copy-start.19
  458.4 7.8 copy-start.24
  458.5 7.8 copy-start.55
  500.2 7.2 copy-start.29
  500.2 7.2 copy-start.30
  500.2 7.2 copy-start.31
  508.2 7.1 copy-start.20
  508.2 7.1 copy-start.56
  508.2 7.0 copy-start.67
  508.2 7.0 copy-start.79
  514.0 6.3 slice-start
  523.6 61.9 %copy-start.74 = (f32[512]{0:T(512)S(1)}, f32[512]{0:T(512)}, u32[]{:S(2)}) copy-start(f32[512]{0:T(512)} %get-tuple-element.55) | copy-start | bytes 6148
  523.6 61.9 %copy-start.73 = (f32[512]{0:T(512)S(1)}, f32[512]{0:T(512)}, u32[]{:S(2)}) copy-start(f32[512]{0:T(512)} %get-tuple-element.56) | copy-start | bytes 6148
  523.6 61.9 %copy-start.8 = (f32[512,768]{1,0:T(8,128)S(1)}, f32[512,768]{1,0:T(8,128)}, u32[]{:S(2)}) copy-start(f32[512,768]{1,0:T(8,128)} %copy-done.7) | copy-start | bytes 4718596
  523.6 61.9 %copy-start.64 = (f32[512]{0:T(512)S(1)}, f32[512]{0:T(512)}, u32[]{:S(2)}) copy-start(f32[512]{0:T(512)} %copy-done.62) | copy-start | bytes 6148
  588.6 9.1 %copy-start.34 = (bf16[24,9344]{1,0:T(8,128)(2,1)S(1)}, bf16[24,9344]{1,0:T(8,128)(2,1)}, u32[]{:S(2)}) copy-start(bf16[24,9344]{1,0:T(8,128)(2,1)} %reduce-scatter.4.cloned.1.call-done) | copy-start | bytes 1345540
  (43 other events, 136.9 us)
Sparse Core Ops, SparseCore 0:
  18.9 106.7 all-gather.4
  129.2 102.2 all-gather.2
  423.5 161.9 reduce-scatter.3
  592.7 248.9 all-reduce.7
